TPU v7x, 32 devices: a whole 2x2x4 slice. The times are simulated.
32 devices in a mesh: pair: 4 (over y, x), ep: 8 (over z, core).
Axes of the slice: x: 2, y: 2, z: 4, core: 2. Of those that a mesh axis runs over, the one named last changes fastest.
Arguments:
- hidden: float32 [4, 256, 2048], P('pair', 'ep'), may hold values from -6 to 6
- moe_gain: float32 [2048], replicated, may hold values from 0.25 to 1.75
- expert_ids: int32 [4, 256, 2], P('pair', 'ep'), may hold values from 0 to 3, all different within a row; in each aligned block of 32 rows (0 to 31, 32 to 63, ..., all dimensions but the last counted through in order) at most 32 rows name the same one
- gate_weights: float32 [4, 256, 2], P('pair', 'ep'), may hold values from 0.2 to 1
- w_gate: bfloat16 [8, 2048, 2048], P('ep', None, 'pair'), may hold values from -0.125 to 0.125
- w_up: bfloat16 [8, 2048, 2048], P('ep', None, 'pair'), may hold values from -0.125 to 0.125
- w_down: bfloat16 [8, 2048, 2048], P('ep', 'pair'), may hold values from -0.09375 to 0.09375
- final_gain: float32 [2048], replicated, may hold values from 0.25 to 1.75
- w_out: bfloat16 [2048, 128], replicated, may hold values from -0.125 to 0.125
- latent: float32 [4, 256, 64], P('pair', 'ep'), may hold values from -6 to 6
- w_in: bfloat16 [128, 2048], replicated, may hold values from -0.5 to 0.5
- modulation: float32 [4, 2, 2048], P('pair'), may hold values from -3 to 16, as said below
- w_qkv: bfloat16 [2048, 3072], P(None, 'pair'), may hold values from -0.125 to 0.125
Outputs:
- latent_next: float32 [4, 256, 64], P('pair', 'ep')
- attended: bfloat16 [4, 256, 1024], P('pair', 'ep')
Inputs may be any that keep to these rules, and one draw needn't show every extreme that they name: `expert_ids`: within the 32 frames of each device no expert is named more than 32 times, a bound that some block reaches; the two experts of a frame differ. `modulation`: row 0 is a shift, row 1 a positive scale.
All inputs are finite; a program needn't handle non-finite values.
Results may differ from a plain program's by a relative error of at most 0.03.
Values may be sent and summed in bfloat16 or wider, within the bound.
A program may use at most 64 MiB of HBM per device.

v0:
```python
import math

import jax
import jax.numpy as jnp
from jax import lax
from jax.sharding import PartitionSpec as P

HDIM = 128


EPSILON = 1e-06
GUIDANCE = 3.0
STEP_SIZE = 0.25


def from_partner(value, axis, bit):
    mask = 2**bit
    pairs = [(source, source ^ mask) for source in range(lax.axis_size(axis))]
    return lax.ppermute(value, axis, pairs)


def rms_scale(values):
    return values * lax.rsqrt(jnp.mean(values * values, -1, keepdims=True) + EPSILON)


def per_device(
    hidden,
    moe_gain,
    expert_ids,
    gate_weights,
    w_gate,
    w_up,
    w_down,
    final_gain,
    w_out,
    latent,
    w_in,
    modulation,
    w_qkv,
):
    tok_rows = hidden.shape[1]
    model_width = hidden.shape[2]
    experts = lax.axis_size("ep") // 2
    capacity = 4 * tok_rows // experts
    slot_count = experts * capacity
    own_hidden = hidden[0]
    normed = (rms_scale(own_hidden) * moe_gain).astype(jnp.bfloat16)
    flat_ids = expert_ids[0].reshape(-1)
    onehot = (flat_ids[:, None] == jnp.arange(experts, dtype=jnp.int32)[None, :]).astype(jnp.int32)
    slot_rank = jnp.sum((jnp.cumsum(onehot, 0) - onehot) * onehot, 1)
    places = flat_ids * capacity + slot_rank
    matches = places[None, :] == jnp.arange(slot_count, dtype=jnp.int32)[:, None]
    dispatch_mat = jnp.sum(matches.reshape(slot_count, tok_rows, 2).astype(jnp.float32), 2).astype(
        jnp.bfloat16
    )
    buffers = jnp.dot(dispatch_mat, normed, preferred_element_type=jnp.float32).astype(jnp.bfloat16)
    doubled = jnp.broadcast_to(
        buffers.reshape(experts, 1, capacity, model_width), (experts, 2, capacity, model_width)
    ).reshape(2 * experts, capacity, model_width)
    arrived = lax.all_to_all(doubled, "ep", split_axis=0, concat_axis=0, tiled=True)
    all_rows = lax.all_gather(arrived.reshape(-1, model_width), "pair", axis=0, tiled=True)
    gate_mat = w_gate[0]
    up_mat = w_up[0]
    down_mat = w_down[0]
    gated = jnp.dot(all_rows, gate_mat, preferred_element_type=jnp.float32)
    upward = jnp.dot(all_rows, up_mat, preferred_element_type=jnp.float32)
    active = (jax.nn.silu(gated) * upward).astype(jnp.bfloat16)
    halves = lax.psum_scatter(
        jnp.dot(active, down_mat, preferred_element_type=jnp.float32).astype(jnp.bfloat16),
        "pair",
        scatter_dimension=0,
        tiled=True,
    )
    returned = lax.all_to_all(
        halves.reshape(2 * experts, capacity, model_width),
        "ep",
        split_axis=0,
        concat_axis=0,
        tiled=True,
    )
    paired = returned.reshape(experts, 2, capacity, model_width)
    summed = (paired[:, 0].astype(jnp.float32) + paired[:, 1].astype(jnp.float32)).reshape(
        slot_count, model_width
    )
    combine_mat = jnp.sum(
        jnp.where(matches, gate_weights[0].reshape(-1)[None, :], 0.0).reshape(
            slot_count, tok_rows, 2
        ),
        2,
    )
    mixed_out = jnp.einsum("st,sd->td", combine_mat, summed, precision=lax.Precision.HIGHEST)
    resid = own_hidden + mixed_out
    velocity = jnp.dot(
        (rms_scale(resid) * final_gain).astype(jnp.bfloat16),
        w_out,
        preferred_element_type=jnp.float32,
    )
    own_latent = latent[0]
    outgoing = jnp.concatenate([velocity, own_latent], 1)
    incoming = from_partner(outgoing, "pair", 0)
    channels = velocity.shape[1]
    partner_vel = incoming[:, :channels]
    partner_latent = incoming[:, channels:]
    is_cond = lax.axis_index("pair") % 2 == 0
    cond_vel = jnp.where(is_cond, velocity, partner_vel)
    uncond_vel = jnp.where(is_cond, partner_vel, velocity)
    guided = uncond_vel + GUIDANCE * (cond_vel - uncond_vel)
    whole_latent = jnp.where(
        is_cond,
        jnp.concatenate([own_latent, partner_latent], 1),
        jnp.concatenate([partner_latent, own_latent], 1),
    )
    advanced = whole_latent + STEP_SIZE * guided
    half_width = own_latent.shape[1]
    own_next = jnp.where(is_cond, advanced[:, :half_width], advanced[:, half_width:])
    embedded = jnp.dot(advanced.astype(jnp.bfloat16), w_in, preferred_element_type=jnp.float32)
    modulated = (rms_scale(embedded) * modulation[0, 1] + modulation[0, 0]).astype(jnp.bfloat16)
    all_modulated = lax.all_gather(modulated, "pair", axis=0, tiled=True)
    local_cols = jnp.dot(all_modulated, w_qkv, preferred_element_type=jnp.float32).astype(
        jnp.bfloat16
    )
    projected = lax.all_to_all(local_cols, "pair", split_axis=0, concat_axis=1, tiled=True)
    head_width = projected.shape[1] // 3
    head_count = head_width // HDIM
    queries = projected[:, :head_width].reshape(tok_rows, head_count, HDIM)
    key_cols = projected[:, head_width : 2 * head_width]
    value_cols = projected[:, 2 * head_width :]
    score_scale = 1.0 / math.sqrt(HDIM)
    running_max = jnp.full((head_count, tok_rows), -1e30, jnp.float32)
    key_piece = lax.all_gather(key_cols, "ep", axis=0, tiled=True).reshape(-1, head_count, HDIM)
    value_piece = lax.all_gather(value_cols, "ep", axis=0, tiled=True).reshape(-1, head_count, HDIM)
    scores = (
        jnp.einsum("thd,nhd->htn", queries, key_piece, preferred_element_type=jnp.float32)
        * score_scale
    )
    new_max = jnp.maximum(running_max, jnp.max(scores, 2))
    weights = jnp.exp(scores - new_max[:, :, None])
    new_sum = jnp.sum(weights, 2)
    new_accum = jnp.einsum(
        "htn,nhd->htd", weights, value_piece.astype(jnp.float32), precision=lax.Precision.HIGHEST
    )
    attended = (
        (new_accum / new_sum[:, :, None])
        .transpose(1, 0, 2)
        .reshape(tok_rows, head_width)
        .astype(jnp.bfloat16)
    )
    return (own_next[None], attended[None])


def solution(mesh):
    return jax.shard_map(
        per_device,
        mesh=mesh,
        in_specs=(
            P("pair", "ep", None),
            P(),
            P("pair", "ep", None),
            P("pair", "ep", None),
            P("ep", None, "pair"),
            P("ep", None, "pair"),
            P("ep", "pair", None),
            P(),
            P(),
            P("pair", "ep", None),
            P(),
            P("pair", None, None),
            P(None, "pair"),
        ),
        out_specs=(P("pair", "ep", None), P("pair", "ep", None)),
        check_vma=False,
    )
```

profile of v0, /device:TPU:0, one launch (start us, length us, event | category | flops | bytes accessed | tf_op | source)
XLA Modules:
  0.0 272.6 jit_solution(4864884305753310262)
XLA Ops:
  7.2 0.0 copy-start
  7.2 0.0 all-gather.2.cloned.1.call-start
  7.2 0.9 copy.41
  8.1 0.1 eq.36
  8.2 0.1 fusion.24
  8.3 0.1 reduce_window_sum.11
  8.4 0.2 select_reduce_fusion.1
  8.6 0.1 reduce_sum.66
  8.7 0.1 copy.42
  8.8 0.7 bitcast_add_fusion
  9.5 1.1 fusion.11
  10.6 0.8 convert_reduce_fusion
  11.3 1.3 convolution_convert_fusion.1
  12.7 0.1 broadcast_in_dim.42
  12.8 32.8 %all_to_all.29 = bf16[8,32,2048]{2,1,0:T(8,128)(2,1)} all-to-all(bf16[8,32,2048]{2,1,0:T(8,128)(2,1)S(1)} %bitcast.71), channel_id=1, replica_groups=mesh['pair'=4,'ep'=8] {'ep'}, dimensions={0} | all-to-all | bytes 2097152 | tf_op jit(solution)/shard_map/all_to_all | solution.py:60
  45.6 0.0 all-gather.2.cloned.1.call-update
  45.6 0.0 reduce-scatter.2.cloned.1.call-start
  45.7 51.7 %all-gather.2.cloned.1.call-done = bf16[1024,2048]{1,0:T(8,128)(2,1)} async-done(((bf16[256,2048]{1,0:T(8,128)(2,1)}), bf16[1024,2048]{1,0:T(8,128)(2,1)}) %all-gather.2.cloned.1.call-update) | async-done | bytes 4194320 | tf_op jit(solution)/shard_map/all_gather | solution.py:61
  97.4 6.6 %fusion.1 = f32[1024,512]{1,0:T(8,128)} fusion(bf16[1024,2048]{1,0:T(8,128)(2,1)} %all-gather.2.cloned.1.call-done, bf16[1,2048,512]{2,1,0:T(8,128)(2,1)} %param.18), kind=kOutput, calls=%fused_computation.4 | convolution fusion | flops 2147483648 | bytes 8388608 | tf_op jit(solution)/shard_map/dot_general | solution.py:66
  104.0 10.7 %convolution_convert_fusion = bf16[1024,2048]{1,0:T(8,128)(2,1)} fusion(bf16[1,512,2048]{2,1,0:T(8,128)(2,1)} %param.19, f32[1024,512]{1,0:T(8,128)} %fusion.1, bf16[1024,2048]{1,0:T(8,128)(2,1)} %all-gather.2.cloned.1.call-done, bf16[1,2048,512]{2,1,0:T(8,128)(2,1)} %param.17), kind=kOutput, calls=%fused_computation | convolution fusion | flops 4300210176 | bytes 14680064 | tf_op jit(solution)/shard_map/dot_general | solution.py:69
  114.7 0.0 reduce-scatter.2.cloned.1.call-update
  114.7 52.9 %reduce-scatter.2.cloned.1.call-done = bf16[256,2048]{1,0:T(8,128)(2,1)} async-done(((bf16[1024,2048]{1,0:T(8,128)(2,1)}), bf16[256,2048]{1,0:T(8,128)(2,1)}) %reduce-scatter.2.cloned.1.call-update) | async-done | bytes 1048592 | tf_op jit(solution)/shard_map/reduce_scatter | solution.py:68
  167.6 31.3 %all_to_all.30 = bf16[8,32,2048]{2,1,0:T(8,128)(2,1)S(1)} all-to-all(bf16[8,32,2048]{2,1,0:T(8,128)(2,1)} %bitcast.75), channel_id=1, replica_groups=mesh['pair'=4,'ep'=8] {'ep'}, dimensions={0} | all-to-all | bytes 2097152 | tf_op jit(solution)/shard_map/all_to_all | solution.py:74
  198.9 0.1 convert_add_fusion
  199.1 0.0 copy-done.1
  199.1 0.8 multiply_reduce_fusion.1
  199.8 0.1 copy-done.2
  200.0 0.0 copy-done.5
  200.0 0.3 fusion.15
  200.2 0.0 copy-done.3
  200.2 1.5 collective-permute-start
  201.7 2.5 collective-permute-done
  204.2 0.1 fusion.26
  204.3 1.4 multiply_reduce_fusion
  205.7 0.1 add_convert_fusion
  205.8 10.6 %all_gather.13 = bf16[128,2048]{1,0:T(8,128)(2,1)S(1)} all-gather(bf16[32,2048]{1,0:T(8,128)(2,1)S(1)} %add_convert_fusion), channel_id=1, replica_groups=mesh['pair'=4,'ep'=8] {'pair'}, dimensions={0}, use_global_device_ids=true | all-gather | bytes 655360 | tf_op jit(solution)/shard_map/all_gather | solution.py:118
  216.4 1.3 convolution_convert_fusion.2
  217.6 3.4 %all-to-all-start.2 = ((bf16[4,32,768]{2,1,0:T(8,128)(2,1)}), bf16[4,32,768]{2,1,0:T(8,128)(2,1)S(1)}, u32[]{:S(2)}, u32[]{:S(2)}) async-start(bf16[4,32,768]{2,1,0:T(8,128)(2,1)} %bitcast.16), calls=%async_computation.3 | async-start | bytes 393216 | tf_op jit(solution)/shard_map/all_to_all | solution.py:122
  221.0 0.7 fusion.25
  221.7 4.5 %all-to-all-done.2 = bf16[4,32,768]{2,1,0:T(8,128)(2,1)S(1)} async-done(((bf16[4,32,768]{2,1,0:T(8,128)(2,1)}), bf16[4,32,768]{2,1,0:T(8,128)(2,1)S(1)}, u32[]{:S(2)}, u32[]{:S(2)}) %all-to-all-start.2) | async-done | bytes 196640 | tf_op jit(solution)/shard_map/all_to_all | solution.py:122
  226.2 15.7 %all_gather.15 = bf16[256,1024]{1,0:T(8,128)(2,1)} all-gather(bf16[32,1024]{1,0:T(8,128)(2,1)S(1)} %get-tuple-element.5), channel_id=1, replica_groups=mesh['pair'=4,'ep'=8] {'ep'}, dimensions={0}, use_global_device_ids=true | all-gather | bytes 589824 | tf_op jit(solution)/shard_map/all_gather | solution.py:131
  241.9 2.0 copy.47
  244.0 15.8 %all_gather.14 = bf16[256,1024]{1,0:T(8,128)(2,1)} all-gather(bf16[32,1024]{1,0:T(8,128)(2,1)S(1)} %get-tuple-element.6), channel_id=1, replica_groups=mesh['pair'=4,'ep'=8] {'ep'}, dimensions={0}, use_global_device_ids=true | all-gather | bytes 589824 | tf_op jit(solution)/shard_map/all_gather | solution.py:130
  259.8 2.1 copy.44
  261.8 1.3 fusion.32
  263.2 0.2 fusion.14
  263.4 1.7 fusion.8
  265.1 0.7 convert_element_type.71
  (17 shorter events, 0.1 us)
Async XLA Ops:
  7.2 209.2 %copy-start = (bf16[2048,768]{1,0:T(8,128)(2,1)S(1)}, bf16[2048,768]{1,0:T(8,128)(2,1)}, u32[]{:S(2)}) copy-start(bf16[2048,768]{1,0:T(8,128)(2,1)} %param.25) | copy-start | bytes 9437188
  7.2 90.2 %all-gather.2.cloned.1.call-start = ((), (), s32[]{:S(2)}) async-start(), calls=%async_computation.4 | async-start | bytes 5242880 | tf_op jit(solution)/shard_map/all_gather | solution.py:61
  45.6 122.0 %reduce-scatter.2.cloned.1.call-start = ((), (), s32[]{:S(2)}) async-start(), calls=%async_computation.5 | async-start | bytes 5242880 | tf_op jit(solution)/shard_map/reduce_scatter | solution.py:68
  167.6 31.5 %copy-start.1 = (f32[1,32,2048]{2,1,0:T(8,128)S(1)}, f32[1,32,2048]{2,1,0:T(8,128)}, u32[]{:S(2)}) copy-start(f32[1,32,2048]{2,1,0:T(8,128)} %param.13) | copy-start | bytes 786436
  198.9 1.0 copy-start.2
  198.9 1.0 copy-start.5
  198.9 1.3 copy-start.3
  198.9 2.8 %copy-start.4 = (f32[1,2,2048]{2,1,0:T(2,128)S(1)}, f32[1,2,2048]{2,1,0:T(2,128)}, u32[]{:S(2)}) copy-start(f32[1,2,2048]{2,1,0:T(2,128)} %param.24) | copy-start | bytes 49156
  200.2 4.0 %collective-permute-start = (f32[32,192]{1,0:T(8,128)S(1)}, f32[32,192]{1,0:T(8,128)S(1)}, u32[]{:S(2)}, u32[]{:S(2)}) collective-permute-start(f32[32,192]{1,0:T(8,128)S(1)} %pad_maximum_fusion), channel_id=1, source_target_pairs={{0,8},{8,0},{16,24},{24,16},{1,9},{9,1},{17,25},{25,17},{2,10},{10... | collective-permute-start | bytes 73736 | tf_op jit(solution)/shard_map/ppermute | solution.py:19
  217.6 8.5 %all-to-all-start.2 = ((bf16[4,32,768]{2,1,0:T(8,128)(2,1)}), bf16[4,32,768]{2,1,0:T(8,128)(2,1)S(1)}, u32[]{:S(2)}, u32[]{:S(2)}) async-start(bf16[4,32,768]{2,1,0:T(8,128)(2,1)} %bitcast.16), calls=%async_computation.3 | async-start | bytes 393216 | tf_op jit(solution)/shard_map/all_to_all | solution.py:122
Sparse Core Ops, SparseCore 0:
  45.7 51.5 all-gather.1
  114.8 52.7 reduce-scatter.1
where the time goes:
time: 273 us
  waiting for transfers between devices  112 us (41%)
  blocking collectives  106 us (39%)
  matrix products  25.2 us (9%)
  between operations  14.2 us (5%)
  local copies, waits for them, and re-layouts  6.28 us (2%)
  starting transfers between devices  4.9 us (2%)
  other arithmetic  4.13 us (2%)
    reduce_scatter x1, waiting for transfers between devices, per_device(): lax.psum_scatter(jnp.dot(active, down_mat, preferred_element_type=jnp.flo...  52.9 us
    all_gather x1, waiting for transfers between devices, per_device(): lax.all_gather(arrived.reshape(-1, model_width), 'pair', axis=0, tiled=True)  51.7 us
    all_to_all x1, blocking collectives, per_device(): lax.all_to_all(doubled, 'ep', split_axis=0, concat_axis=0, tiled=True)  32.8 us
    all_to_all x1, blocking collectives, per_device(): lax.all_to_all(halves.reshape(2 * experts, capacity, model_width), 'ep',...  31.3 us
    all_gather x1, blocking collectives, per_device(): lax.all_gather(key_cols, 'ep', axis=0, tiled=True)  15.8 us
    all_gather x1, blocking collectives, per_device(): lax.all_gather(value_cols, 'ep', axis=0, tiled=True)  15.7 us
    dot_general x1, matrix products, per_device(): jnp.dot(active, down_mat, preferred_element_type=jnp.float32)  10.7 us
    all_gather x1, blocking collectives, per_device(): all_modulated = lax.all_gather(modulated, 'pair', axis=0, tiled=True)  10.6 us
  transfers between devices with their start and end apart: 4, of which 4 were waited for; matrix products, arithmetic and copies ran while one was open for 0% of the time, Pallas kernels for 0%

commit v1 on v0

--- a/solution.py
+++ b/solution.py
@@ -3,6 +3,8 @@
 import jax
 import jax.numpy as jnp
 from jax import lax
+from jax.experimental import pallas as pl
+from jax.experimental.pallas import tpu as pltpu
 from jax.sharding import PartitionSpec as P
 
 HDIM = 128
@@ -148,9 +150,488 @@
     return (own_next[None], attended[None])
 
 
+Z_IN, X_IN, Y_IN, XY_IN, YX_IN, CORE_IN = 0, 1, 2, 3, 4, 5
+CORE_OUT, XD_OUT, YD_OUT, X_OUT, Y_OUT, Z_OUT = 9, 10, 11, 12, 13, 14
+KINDS = 15
+
+
+def fused_kernel(
+    hid,
+    moe_gain,
+    ids,
+    gates,
+    gate_hbm,
+    up_hbm,
+    down_hbm,
+    final_gain,
+    out_hbm,
+    lat,
+    in_hbm,
+    mod,
+    qkv_hbm,
+    next_ref,
+    att_ref,
+    rows,
+    wg,
+    wu,
+    wd,
+    wout,
+    win,
+    wqkv,
+    act,
+    sums,
+    core_send,
+    core_recv,
+    diag_send,
+    diag_recv,
+    side_send,
+    side_recv,
+    z_send,
+    z_recv,
+    lats,
+    mods,
+    vels,
+    cols,
+    qkv,
+    heads,
+    whole,
+    load_sem,
+    send_sem,
+    recv_sem,
+    small_send,
+    small_recv,
+    col_send,
+    col_recv,
+    head_send,
+    head_recv,
+):
+    p, ep = lax.axis_index("pair"), lax.axis_index("ep")
+    x, y = lax.rem(p, 2), lax.div(p, 2)
+    core, z = lax.rem(ep, 2), lax.div(ep, 2)
+    px, py = y * 2 + (1 - x), (1 - y) * 2 + x
+    pd = (1 - y) * 2 + (1 - x)
+    pairs = (p, px, py, pd)
+    core_ep = z * 2 + (1 - core)
+    tok = hid.shape[1]
+    half = tok // 2
+    hidden_units = wg.shape[1]
+    width = wd.shape[1]
+
+    def place(k):
+        low = lax.rem(lax.rem(z, 2) + lax.rem(k, 2), 2)
+        high = lax.rem(lax.div(z, 2) + lax.div(k, 2), 2)
+        return high * 2 + low
+
+    def copy(src, dst, sent, received, device):
+        return pltpu.make_async_remote_copy(
+            src_ref=src,
+            dst_ref=dst,
+            send_sem=sent,
+            recv_sem=received,
+            device_id=device,
+            device_id_type=pl.DeviceIdType.MESH,
+        )
+
+    top, low = pl.ds(0, half), pl.ds(half, half)
+
+    def group(kind, k):
+        if kind == Z_IN:
+            src, dst, dev = rows.at[0, 0, 0], rows.at[k, 0, 0], (p, place(k) * 2 + core)
+        elif kind == X_IN:
+            src, dst, dev = rows.at[k, 0, 0], rows.at[k, 0, 1], (px, ep)
+        elif kind == Y_IN:
+            src, dst, dev = rows.at[k, 0, 0], rows.at[k, 0, 2], (py, ep)
+        elif kind == XY_IN:
+            src, dst, dev = rows.at[k, 0, 1, top], rows.at[k, 0, 3, top], (py, ep)
+        elif kind == YX_IN:
+            src, dst, dev = rows.at[k, 0, 2, low], rows.at[k, 0, 3, low], (px, ep)
+        elif kind < CORE_OUT:
+            r = kind - CORE_IN
+            src, dst, dev = rows.at[k, 0, r], rows.at[k, 1, r], (p, core_ep)
+        elif kind == CORE_OUT:
+            src, dst, dev = core_send.at[k], core_recv.at[k], (p, core_ep)
+        elif kind == XD_OUT:
+            src, dst, dev = diag_send.at[k, 0], diag_recv.at[k, 0], (px, ep)
+        elif kind == YD_OUT:
+            src, dst, dev = diag_send.at[k, 1], diag_recv.at[k, 1], (py, ep)
+        elif kind == X_OUT:
+            src, dst, dev = side_send.at[k, 0], side_recv.at[k, 0], (px, ep)
+        elif kind == Y_OUT:
+            src, dst, dev = side_send.at[k, 1], side_recv.at[k, 1], (py, ep)
+        else:
+            src, dst, dev = z_send.at[k], z_recv.at[k], (p, place(k) * 2 + core)
+        return copy(src, dst, send_sem.at[kind, k], recv_sem.at[kind, k], dev)
+
+    loads = [
+        pltpu.make_async_copy(src, dst, load_sem.at[i])
+        for i, (src, dst) in enumerate(
+            (
+                (gate_hbm.at[0], wg),
+                (up_hbm.at[0], wu),
+                (down_hbm.at[0], wd),
+                (out_hbm, wout),
+                (in_hbm, win),
+                (qkv_hbm, wqkv),
+            )
+        )
+    ]
+
+    rows[0, 0, 0] = (rms_scale(hid[0]) * moe_gain[...]).astype(jnp.bfloat16)
+    for k in range(1, 4):
+        group(Z_IN, k).start()
+    for load in loads:
+        load.start()
+    lats[0] = jnp.zeros_like(lats[0])
+    lats[0, :, : lat.shape[2]] = lat[0]
+    mods[0] = mod[0]
+
+    def small(kind, r):
+        buffer = (lats, mods, vels)[kind]
+        return copy(
+            buffer.at[0],
+            buffer.at[r],
+            small_send.at[kind, r],
+            small_recv.at[kind, r],
+            (pairs[r], ep),
+        )
+
+    def spread(k):
+        @pl.when(k > 0)
+        def _():
+            group(Z_IN, k).wait_recv()
+
+        group(X_IN, k).start()
+        group(Y_IN, k).start()
+        group(CORE_IN, k).start()
+        group(X_IN, k).wait_recv()
+        group(XY_IN, k).start()
+        group(CORE_IN + 1, k).start()
+        group(Y_IN, k).wait_recv()
+        group(YX_IN, k).start()
+        group(CORE_IN + 2, k).start()
+
+    def experts(k):
+        group(XY_IN, k).wait_recv()
+        group(YX_IN, k).wait_recv()
+        group(CORE_IN + 3, k).start()
+        for r in range(4):
+            group(CORE_IN + r, k).wait_recv()
+
+        @pl.when(k == 0)
+        def _():
+            for load in loads[:3]:
+                load.wait()
+
+        own = rows[k].reshape(8 * tok, width)
+        step = min(256, hidden_units)
+        for at in range(0, hidden_units, step):
+            gated = jnp.dot(own, wg[:, at : at + step], preferred_element_type=jnp.float32)
+            upward = jnp.dot(own, wu[:, at : at + step], preferred_element_type=jnp.float32)
+            act[:, at : at + step] = (jax.nn.silu(gated) * upward).astype(jnp.bfloat16)
+        step = min(512, width)
+        for at in range(0, width, step):
+            part = jnp.dot(act[...], wd[:, at : at + step], preferred_element_type=jnp.float32)
+            part = part.reshape(2, 4, tok, step)
+            sums[k, :, :, at : at + step] = part[0]
+            core_send[k, :, :, at : at + step] = part[1].astype(jnp.bfloat16)
+        group(CORE_OUT, k).start()
+
+    def join_cores(k):
+        group(CORE_OUT, k).wait_recv()
+        diag = sums[k, 3] + core_recv[k, 3].astype(jnp.float32)
+        diag_send[k] = diag.astype(jnp.bfloat16).reshape(2, half, width)
+        group(XD_OUT, k).start()
+        group(YD_OUT, k).start()
+        for r in range(3):
+            sums[k, r] = sums[k, r] + core_recv[k, r].astype(jnp.float32)
+
+    def join_diagonal(k):
+        group(XD_OUT, k).wait_recv()
+        group(YD_OUT, k).wait_recv()
+        side_send[k, 0, :half] = sums[k, 1, :half].astype(jnp.bfloat16)
+        side_send[k, 0, half:] = (
+            sums[k, 1, half:] + diag_recv[k, 1].astype(jnp.float32)
+        ).astype(jnp.bfloat16)
+        group(X_OUT, k).start()
+        side_send[k, 1, :half] = (
+            sums[k, 2, :half] + diag_recv[k, 0].astype(jnp.float32)
+        ).astype(jnp.bfloat16)
+        side_send[k, 1, half:] = sums[k, 2, half:].astype(jnp.bfloat16)
+        group(Y_OUT, k).start()
+
+    def join_sides(k):
+        group(X_OUT, k).wait_recv()
+        group(Y_OUT, k).wait_recv()
+        total = (
+            sums[k, 0]
+            + side_recv[k, 0].astype(jnp.float32)
+            + side_recv[k, 1].astype(jnp.float32)
+        ).astype(jnp.bfloat16)
+
+        @pl.when(k == 0)
+        def _():
+            z_recv[0] = total
+
+        @pl.when(k > 0)
+        def _():
+            z_send[k] = total
+            group(Z_OUT, k).start()
+
+    stages = ((spread, 0), (experts, 1), (join_cores, 2), (join_diagonal, 3), (join_sides, 4))
+
+    def turn(it, carry):
+        for stage, lag in stages:
+
+            @pl.when((it >= lag) & (it < lag + 4))
+            def _(stage=stage, lag=lag):
+                stage(it - lag)
+
+        @pl.when(it == 0)
+        def _():
+            for r in range(1, 4):
+                small(0, r).start()
+                small(1, r).start()
+
+        return carry
+
+    lax.fori_loop(0, 8, turn, 0)
+
+    mixed = jnp.zeros((tok, width), jnp.float32)
+    for k in range(4):
+        if k > 0:
+            group(Z_OUT, k).wait_recv()
+        weight = jnp.sum(jnp.where(ids[0] == place(k), gates[0], 0.0), 1, keepdims=True)
+        mixed = mixed + weight * z_recv[k].astype(jnp.float32)
+    resid = hid[0] + mixed
+    loads[3].wait()
+    vels[0] = jnp.dot(
+        (rms_scale(resid) * final_gain[...]).astype(jnp.bfloat16),
+        wout[...],
+        preferred_element_type=jnp.float32,
+    )
+    for r in range(1, 4):
+        small(2, r).start()
+    for kind in range(3):
+        for r in range(1, 4):
+            small(kind, r).wait_recv()
+
+    is_cond = x == 0
+    half_channels = lat.shape[2]
+
+    def advance(first, second):
+        cond_vel = jnp.where(is_cond, vels[first], vels[second])
+        uncond_vel = jnp.where(is_cond, vels[second], vels[first])
+        cond_lat = jnp.where(is_cond, lats[first], lats[second])[:, :half_channels]
+        uncond_lat = jnp.where(is_cond, lats[second], lats[first])[:, :half_channels]
+        guided = uncond_vel + GUIDANCE * (cond_vel - uncond_vel)
+        return jnp.concatenate([cond_lat, uncond_lat], 1) + STEP_SIZE * guided
+
+    advanced = advance(0, 1)
+    next_ref[0] = jnp.where(is_cond, advanced[:, :half_channels], advanced[:, half_channels:])
+    both = jnp.concatenate([advanced, advance(2, 3)], 0).astype(jnp.bfloat16)
+    loads[4].wait()
+    scaled = rms_scale(jnp.dot(both, win[...], preferred_element_type=jnp.float32))
+    modulated = jnp.concatenate(
+        [
+            (scaled[(r // 2) * tok : (r // 2 + 1) * tok] * mods[r, 1:2] + mods[r, 0:1]).astype(
+                jnp.bfloat16
+            )
+            for r in range(4)
+        ],
+        0,
+    )
+    loads[5].wait()
+    local = jnp.dot(modulated, wqkv[...], preferred_element_type=jnp.float32).astype(jnp.bfloat16)
+    blocks = local.shape[1] // HDIM
+    for r in range(4):
+        for b in range(blocks):
+            cols[r, b] = local[r * tok : (r + 1) * tok, b * HDIM : (b + 1) * HDIM]
+
+    def column(r, b):
+        number = p * blocks + b
+        sort, head = lax.div(number, 8), lax.rem(number, 8)
+        return head, sort, copy(
+            cols.at[r, b],
+            qkv.at[sort, ep],
+            col_send.at[r, b],
+            col_recv.at[sort, ep],
+            (pairs[r], head),
+        )
+
+    def each_column(act_on, keep):
+        for r in (3, 1, 2, 0):
+            for b in range(blocks):
+                head, sort, moved = column(r, b)
+                if r > 0:
+                    act_on(moved)
+                    continue
+
+                @pl.when(head != ep)
+                def _(moved=moved):
+                    act_on(moved)
+
+                if keep:
+
+                    @pl.when(head == ep)
+                    def _(sort=sort, b=b):
+                        qkv[sort, ep] = cols[0, b]
+
+    each_column(lambda moved: moved.start(), True)
+    for sort in range(3):
+        for j in range(8):
+
+            @pl.when((lax.div(sort * 8 + ep, blocks) != p) | (ep != j))
+            def _(sort=sort, j=j):
+                copy(
+                    qkv.at[sort, j],
+                    qkv.at[sort, j],
+                    col_send.at[0, 0],
+                    col_recv.at[sort, j],
+                    (px, ep),
+                ).wait_recv()
+
+    query, key, value = (qkv[sort].reshape(8 * tok, HDIM) for sort in range(3))
+    scores = lax.dot_general(
+        query, key, (((1,), (1,)), ((), ())), preferred_element_type=jnp.float32
+    ) * (1.0 / math.sqrt(HDIM))
+    weights = jnp.exp(scores - jnp.max(scores, 1, keepdims=True))
+    total = jnp.sum(weights, 1, keepdims=True)
+    mixed_values = jnp.dot(
+        weights.astype(jnp.bfloat16), value, preferred_element_type=jnp.float32
+    )
+    heads[...] = (mixed_values / total).astype(jnp.bfloat16).reshape(8, tok, HDIM)
+
+    def result(d):
+        j = lax.rem(ep + d, 8)
+        return copy(heads.at[j], whole.at[ep], head_send.at[d], head_recv.at[d], (p, j))
+
+    for d in range(1, 8):
+        result(d).start()
+    whole[ep] = heads[ep]
+    for d in range(1, 8):
+        j = lax.rem(ep + 8 - d, 8)
+        copy(whole.at[j], whole.at[j], head_send.at[d], head_recv.at[d], (px, ep)).wait_recv()
+    for h in range(8):
+        att_ref[0, :, h * HDIM : (h + 1) * HDIM] = whole[h]
+
+    def settle(k, carry):
+        for kind in range(KINDS):
+            if kind in (Z_IN, Z_OUT):
+
+                @pl.when(k > 0)
+                def _(kind=kind):
+                    group(kind, k).wait_send()
+
+            else:
+                group(kind, k).wait_send()
+        return carry
+
+    lax.fori_loop(0, 4, settle, 0)
+    for kind in range(3):
+        for r in range(1, 4):
+            small(kind, r).wait_send()
+    each_column(lambda moved: moved.wait_send(), False)
+    for d in range(1, 8):
+        result(d).wait_send()
+
+
+def fused(
+    hidden,
+    moe_gain,
+    expert_ids,
+    gate_weights,
+    w_gate,
+    w_up,
+    w_down,
+    final_gain,
+    w_out,
+    latent,
+    w_in,
+    modulation,
+    w_qkv,
+):
+    tok, width = hidden.shape[1:]
+    units = w_gate.shape[2]
+    channels = w_out.shape[1]
+    columns = w_qkv.shape[1]
+    blocks = columns // HDIM
+    b16, f32 = jnp.bfloat16, jnp.float32
+    vmem, hbm = pl.BlockSpec(memory_space=pltpu.VMEM), pl.BlockSpec(memory_space=pl.ANY)
+    dma = pltpu.SemaphoreType.DMA
+    half = tok // 2
+    return pl.pallas_call(
+        fused_kernel,
+        out_shape=(
+            jax.ShapeDtypeStruct(latent.shape, f32),
+            jax.ShapeDtypeStruct((1, tok, 8 * HDIM), b16),
+        ),
+        in_specs=[vmem] * 4 + [hbm] * 3 + [vmem, hbm, vmem, hbm, vmem, hbm],
+        out_specs=(vmem, vmem),
+        scratch_shapes=[
+            pltpu.VMEM((4, 2, 4, tok, width), b16),
+            pltpu.VMEM((width, units), b16),
+            pltpu.VMEM((width, units), b16),
+            pltpu.VMEM((units, width), b16),
+            pltpu.VMEM(w_out.shape, b16),
+            pltpu.VMEM(w_in.shape, b16),
+            pltpu.VMEM(w_qkv.shape, b16),
+            pltpu.VMEM((8 * tok, units), b16),
+            pltpu.VMEM((4, 4, tok, width), f32),
+            pltpu.VMEM((4, 4, tok, width), b16),
+            pltpu.VMEM((4, 4, tok, width), b16),
+            pltpu.VMEM((4, 2, half, width), b16),
+            pltpu.VMEM((4, 2, half, width), b16),
+            pltpu.VMEM((4, 2, tok, width), b16),
+            pltpu.VMEM((4, 2, tok, width), b16),
+            pltpu.VMEM((4, tok, width), b16),
+            pltpu.VMEM((4, tok, width), b16),
+            pltpu.VMEM((4, tok, channels), f32),
+            pltpu.VMEM((4, 2, width), f32),
+            pltpu.VMEM((4, tok, channels), f32),
+            pltpu.VMEM((4, blocks, tok, HDIM), b16),
+            pltpu.VMEM((3, 8, tok, HDIM), b16),
+            pltpu.VMEM((8, tok, HDIM), b16),
+            pltpu.VMEM((8, tok, HDIM), b16),
+            dma((6,)),
+            dma((KINDS, 4)),
+            dma((KINDS, 4)),
+            dma((3, 4)),
+            dma((3, 4)),
+            dma((4, blocks)),
+            dma((3, 8)),
+            dma((8,)),
+            dma((8,)),
+        ],
+        compiler_params=pltpu.CompilerParams(
+            has_side_effects=True, vmem_limit_bytes=52 * 2**20
+        ),
+        name="guided_step",
+    )(
+        hidden,
+        moe_gain[None],
+        expert_ids,
+        gate_weights,
+        w_gate,
+        w_up,
+        w_down,
+        final_gain[None],
+        w_out,
+        latent,
+        w_in,
+        modulation,
+        w_qkv,
+    )
+
+
+def choose(mesh):
+    if mesh.shape["pair"] == 4 and mesh.shape["ep"] == 8:
+        return fused
+    return per_device
+
+
 def solution(mesh):
     return jax.shard_map(
-        per_device,
+        choose(mesh),
         mesh=mesh,
         in_specs=(
             P("pair", "ep", None),

time: 273 us -> 94.7 us (0.35)
  waiting for transfers between devices: 112 us -> 0 us
  blocking collectives: 106 us -> 0 us
  Pallas kernels: 0 us -> 84.9 us
  matrix products: 25.2 us -> 0 us
  between operations: 14.2 us -> 0.65 us
  starting transfers between devices: 4.9 us -> 0 us
  other arithmetic: 4.13 us -> 0 us
    pallas_call x0 -> x1, Pallas kernels: none -> 84.9 us  [fused(): pl.pallas_call(fused_kernel, out_shape=(jax.ShapeDtypeStruct(latent.shape...]
    all_to_all x2 -> x0, blocking collectives: 64.1 us -> none  [the longest x1 32.8 us: per_device(): lax.all_to_all(doubled, 'ep', split_axis=0, concat_axis=0, tiled=True)]
    reduce_scatter x1 -> x0, waiting for transfers between devices: 52.9 us -> none  [per_device(): lax.psum_scatter(jnp.dot(active, down_mat, preferred_element_type=jnp.flo...]
    all_gather x1 -> x0, waiting for transfers between devices: 51.7 us -> none  [per_device(): lax.all_gather(arrived.reshape(-1, model_width), 'pair', axis=0, tiled=True)]
    all_gather x3 -> x0, blocking collectives: 42.1 us -> none  [the longest x1 15.8 us: per_device(): lax.all_gather(key_cols, 'ep', axis=0, tiled=True)]
    dot_general x9 -> x0, matrix products: 25.2 us -> none  [the longest x1 10.7 us: per_device(): jnp.dot(active, down_mat, preferred_element_type=jnp.float32)]
    unnamed x14 -> x18, local copies, waits for them, and re-layouts: 1.07 us -> 8.61 us
    all_to_all x1 -> x0, waiting for transfers between devices: 4.48 us -> none  [per_device(): lax.all_to_all(local_cols, 'pair', split_axis=0, concat_axis=1, tiled=True)]
  transfers between devices with their start and end apart: 4 -> 0, of which waited for: 4 -> 0; matrix products, arithmetic and copies ran while one was open for 0% -> 0% of each run, Pallas kernels for 0% -> 0%
where the time goes in v1:
time: 94.7 us; the launch traced here: 94.2 us
  Pallas kernels  84.9 us (90%)
  local copies, waits for them, and re-layouts  8.61 us (9%)
    pallas_call x1, Pallas kernels, fused(): pl.pallas_call(fused_kernel, out_shape=(jax.ShapeDtypeStruct(latent.shape...  84.9 us
    unnamed x18, local copies, waits for them, and re-layouts  8.61 us

profile of v1, /device:TPU:0, one launch (start us, length us, event | category | flops | bytes accessed | tf_op | source)
XLA Modules:
  0.0 94.2 jit_solution(14604603477820410134)
XLA Ops:
  0.6 0.8 copy.15.ids
  1.4 0.8 copy.16.gates
  2.1 0.0 copy-start
  2.2 1.0 %copy-done = bf16[2048,128]{1,0:T(8,128)(2,1)S(1)} copy-done((bf16[2048,128]{1,0:T(8,128)(2,1)S(1)}, bf16[2048,128]{1,0:T(8,128)(2,1)}, u32[]{:S(2)}) %copy-start) | copy-done | bytes 524312
  3.2 0.0 copy-start.1
  3.2 1.0 %copy-done.1 = bf16[128,2048]{1,0:T(8,128)(2,1)S(1)} copy-done((bf16[128,2048]{1,0:T(8,128)(2,1)S(1)}, bf16[128,2048]{1,0:T(8,128)(2,1)}, u32[]{:S(2)}) %copy-start.1) | copy-done | bytes 524312
  4.2 0.0 copy-start.2
  4.2 0.9 %copy-done.2 = f32[1,32,2048]{2,1,0:T(8,128)S(1)} copy-done((f32[1,32,2048]{2,1,0:T(8,128)S(1)}, f32[1,32,2048]{2,1,0:T(8,128)}, u32[]{:S(2)}) %copy-start.2) | copy-done | bytes 262168
  5.2 0.0 copy-start.3
  5.2 0.7 copy-done.3
  5.9 0.0 copy-start.4
  5.9 0.7 copy-done.4
  6.6 0.0 copy-start.5
  6.6 0.7 copy-done.5
  7.3 0.0 copy-start.6
  7.3 0.7 copy-done.6
  8.0 84.9 %guided_step.1 = (f32[1,32,64]{2,1,0:T(8,128)S(1)}, bf16[1,32,1024]{2,1,0:T(8,128)(2,1)S(1)}) custom-call(f32[1,32,2048]{2,1,0:T(8,128)S(1)} %copy-done.2, f32[1,2048]{1,0:T(1,128)S(1)} %bitcast.2, s32[1,32,2]{2,1,0:T(8,128)S(1)} %copy.15.ids, f32[1,32,2]{2,1,0:T(8,128)S(1)} %copy.16.gates, bf16[1,2048,512]{2,1,0:T(8,128)(2,1)} %gate_hbm.1, ...), custom_call_target="tpu_custom_call" | custom-call | tf_op jit(solution)/shard_map/guided_step/pallas_call | solution.py:562
  92.9 0.6 copy.19
  93.5 0.6 copy.20
Async XLA Ops:
  2.1 1.0 %copy-start = (bf16[2048,128]{1,0:T(8,128)(2,1)S(1)}, bf16[2048,128]{1,0:T(8,128)(2,1)}, u32[]{:S(2)}) copy-start(bf16[2048,128]{1,0:T(8,128)(2,1)} %out_hbm.1) | copy-start | bytes 1572868
  3.2 1.0 %copy-start.1 = (bf16[128,2048]{1,0:T(8,128)(2,1)S(1)}, bf16[128,2048]{1,0:T(8,128)(2,1)}, u32[]{:S(2)}) copy-start(bf16[128,2048]{1,0:T(8,128)(2,1)} %in_hbm.1) | copy-start | bytes 1572868
  4.2 0.9 %copy-start.2 = (f32[1,32,2048]{2,1,0:T(8,128)S(1)}, f32[1,32,2048]{2,1,0:T(8,128)}, u32[]{:S(2)}) copy-start(f32[1,32,2048]{2,1,0:T(8,128)} %hid.1) | copy-start | bytes 786436
  5.2 0.7 copy-start.3
  5.9 0.7 copy-start.4
  6.6 0.7 copy-start.5
  7.3 0.7 copy-start.6

commit v2 on v1

--- a/solution.py
+++ b/solution.py
@@ -156,21 +156,27 @@
 
 
 def fused_kernel(
+    hid_hbm,
+    moe_gain_hbm,
+    ids_hbm,
+    gates_hbm,
+    gate_hbm,
+    up_hbm,
+    down_hbm,
+    final_gain_hbm,
+    out_hbm,
+    lat_hbm,
+    in_hbm,
+    mod_hbm,
+    qkv_hbm,
+    next_ref,
+    att_ref,
     hid,
     moe_gain,
     ids,
     gates,
-    gate_hbm,
-    up_hbm,
-    down_hbm,
     final_gain,
-    out_hbm,
     lat,
-    in_hbm,
-    mod,
-    qkv_hbm,
-    next_ref,
-    att_ref,
     rows,
     wg,
     wu,
@@ -195,6 +201,7 @@
     qkv,
     heads,
     whole,
+    early_sem,
     load_sem,
     send_sem,
     recv_sem,
@@ -206,6 +213,35 @@
     head_recv,
 ):
     p, ep = lax.axis_index("pair"), lax.axis_index("ep")
+    barrier = pltpu.get_barrier_semaphore()
+
+    def greet(d, carry):
+        other = lax.rem(p * 8 + ep + d, 32)
+        pl.semaphore_signal(
+            barrier,
+            inc=1,
+            device_id=(lax.div(other, 8), lax.rem(other, 8)),
+            device_id_type=pl.DeviceIdType.MESH,
+        )
+        return carry
+
+    early = [
+        pltpu.make_async_copy(src, dst, early_sem.at[i])
+        for i, (src, dst) in enumerate(
+            (
+                (hid_hbm, hid),
+                (moe_gain_hbm, moe_gain),
+                (ids_hbm, ids),
+                (gates_hbm, gates),
+                (final_gain_hbm, final_gain),
+                (lat_hbm, lat),
+                (mod_hbm.at[0], mods.at[0]),
+            )
+        )
+    ]
+    for load in early:
+        load.start()
+    lax.fori_loop(1, 32, greet, 0)
     x, y = lax.rem(p, 2), lax.div(p, 2)
     core, z = lax.rem(ep, 2), lax.div(ep, 2)
     px, py = y * 2 + (1 - x), (1 - y) * 2 + x
@@ -276,14 +312,14 @@
         )
     ]
 
-    rows[0, 0, 0] = (rms_scale(hid[0]) * moe_gain[...]).astype(jnp.bfloat16)
-    for k in range(1, 4):
-        group(Z_IN, k).start()
     for load in loads:
         load.start()
+    for load in early:
+        load.wait()
+    rows[0, 0, 0] = (rms_scale(hid[0]) * moe_gain[...]).astype(jnp.bfloat16)
     lats[0] = jnp.zeros_like(lats[0])
     lats[0, :, : lat.shape[2]] = lat[0]
-    mods[0] = mod[0]
+    pl.semaphore_wait(barrier, 31)
 
     def small(kind, r):
         buffer = (lats, mods, vels)[kind]
@@ -302,7 +338,19 @@
 
         group(X_IN, k).start()
         group(Y_IN, k).start()
+
+        @pl.when(k == 0)
+        def _():
+            group(Z_IN, 1).start()
+            group(Z_IN, 2).start()
+
+        @pl.when(k == 1)
+        def _():
+            group(Z_IN, 3).start()
+
         group(CORE_IN, k).start()
+
+    def forward(k):
         group(X_IN, k).wait_recv()
         group(XY_IN, k).start()
         group(CORE_IN + 1, k).start()
@@ -377,7 +425,14 @@
             z_send[k] = total
             group(Z_OUT, k).start()
 
-    stages = ((spread, 0), (experts, 1), (join_cores, 2), (join_diagonal, 3), (join_sides, 4))
+    stages = (
+        (spread, 0),
+        (forward, 1),
+        (join_cores, 3),
+        (join_sides, 4),
+        (experts, 2),
+        (join_diagonal, 3),
+    )
 
     def turn(it, carry):
         for stage, lag in stages:
@@ -397,10 +452,14 @@
     lax.fori_loop(0, 8, turn, 0)
 
     mixed = jnp.zeros((tok, width), jnp.float32)
+    eye = lax.broadcasted_iota(jnp.int32, (tok, tok), 0) == lax.broadcasted_iota(
+        jnp.int32, (tok, tok), 1
+    )
     for k in range(4):
         if k > 0:
             group(Z_OUT, k).wait_recv()
-        weight = jnp.sum(jnp.where(ids[0] == place(k), gates[0], 0.0), 1, keepdims=True)
+        weight = jnp.sum(jnp.where(ids[0] == place(k), gates[0], 0.0), 0, keepdims=True)
+        weight = jnp.sum(jnp.where(eye, weight, 0.0), 1, keepdims=True)
         mixed = mixed + weight * z_recv[k].astype(jnp.float32)
     resid = hid[0] + mixed
     loads[3].wait()
@@ -565,9 +624,15 @@
             jax.ShapeDtypeStruct(latent.shape, f32),
             jax.ShapeDtypeStruct((1, tok, 8 * HDIM), b16),
         ),
-        in_specs=[vmem] * 4 + [hbm] * 3 + [vmem, hbm, vmem, hbm, vmem, hbm],
+        in_specs=[hbm] * 13,
         out_specs=(vmem, vmem),
         scratch_shapes=[
+            pltpu.VMEM(hidden.shape, f32),
+            pltpu.VMEM((1, width), f32),
+            pltpu.VMEM((1, 2, tok), jnp.int32),
+            pltpu.VMEM((1, 2, tok), f32),
+            pltpu.VMEM((1, width), f32),
+            pltpu.VMEM(latent.shape, f32),
             pltpu.VMEM((4, 2, 4, tok, width), b16),
             pltpu.VMEM((width, units), b16),
             pltpu.VMEM((width, units), b16),
@@ -592,6 +657,7 @@
             pltpu.VMEM((3, 8, tok, HDIM), b16),
             pltpu.VMEM((8, tok, HDIM), b16),
             pltpu.VMEM((8, tok, HDIM), b16),
+            dma((7,)),
             dma((6,)),
             dma((KINDS, 4)),
             dma((KINDS, 4)),
@@ -603,14 +669,14 @@
             dma((8,)),
         ],
         compiler_params=pltpu.CompilerParams(
-            has_side_effects=True, vmem_limit_bytes=52 * 2**20
+            collective_id=0, has_side_effects=True, vmem_limit_bytes=60 * 2**20
         ),
         name="guided_step",
     )(
         hidden,
         moe_gain[None],
-        expert_ids,
-        gate_weights,
+        expert_ids.transpose(0, 2, 1),
+        gate_weights.transpose(0, 2, 1),
         w_gate,
         w_up,
         w_down,

time: 94.7 us -> 83.4 us (0.88)
  local copies, waits for them, and re-layouts: 8.61 us -> 2.8 us
  Pallas kernels: 84.9 us -> 79.7 us
    unnamed x18 -> x2, local copies, waits for them, and re-layouts: 8.61 us -> 2.8 us
    pallas_call x1, Pallas kernels: 84.9 us -> 79.7 us  [fused(): pl.pallas_call(fused_kernel, out_shape=(jax.ShapeDtypeStruct(latent.shape...]
where the time goes in v2:
time: 83.4 us; the launch traced here: 83.1 us
  Pallas kernels  79.7 us (96%)
  local copies, waits for them, and re-layouts  2.8 us (3%)
    pallas_call x1, Pallas kernels, fused(): pl.pallas_call(fused_kernel, out_shape=(jax.ShapeDtypeStruct(latent.shape...  79.7 us
    unnamed x2, local copies, waits for them, and re-layouts  2.8 us

profile of v2, /device:TPU:0, one launch (start us, length us, event | category | flops | bytes accessed | tf_op | source)
XLA Modules:
  0.0 83.1 jit_solution(10324493471541005257)
XLA Ops:
  0.6 79.7 %guided_step.1 = (f32[1,32,64]{2,1,0:T(8,128)}, bf16[1,32,1024]{2,1,0:T(8,128)(2,1)}) custom-call(f32[1,32,2048]{2,1,0:T(8,128)} %hid_hbm.1, f32[1,2048]{1,0:T(1,128)} %bitcast.4, s32[1,2,32]{2,1,0:T(2,128)} %bitcast.6, f32[1,2,32]{2,1,0:T(2,128)} %bitcast.7, bf16[1,2048,512]{2,1,0:T(8,128)(2,1)} %gate_hbm.1, bf16[1,2048,512]{2,1,0:T(8,128)(2,1)} %up_hbm.1, ...), custom_call_target="tpu_custom_call" | custom-call | tf_op jit(solution)/shard_map/guided_step/pallas_call | solution.py:621
  80.3 1.3 %copy.17 = f32[1,32,64]{2,1,0:T(8,128)} copy(f32[1,32,64]{2,1,0:T(8,128)} %get-tuple-element.4) | data formatting | bytes 16384
  81.7 1.5 %copy.18 = bf16[1,32,1024]{2,1,0:T(8,128)(2,1)} copy(bf16[1,32,1024]{2,1,0:T(8,128)(2,1)} %get-tuple-element.5) | data formatting | bytes 131072

commit v3 on v2

--- a/solution.py
+++ b/solution.py
@@ -344,10 +344,6 @@
             group(Z_IN, 1).start()
             group(Z_IN, 2).start()
 
-        @pl.when(k == 1)
-        def _():
-            group(Z_IN, 3).start()
-
         group(CORE_IN, k).start()
 
     def forward(k):
@@ -425,31 +421,47 @@
             z_send[k] = total
             group(Z_OUT, k).start()
 
-    stages = (
-        (spread, 0),
-        (forward, 1),
-        (join_cores, 3),
-        (join_sides, 4),
-        (experts, 2),
-        (join_diagonal, 3),
-    )
-
-    def turn(it, carry):
-        for stage, lag in stages:
-
-            @pl.when((it >= lag) & (it < lag + 4))
-            def _(stage=stage, lag=lag):
-                stage(it - lag)
-
-        @pl.when(it == 0)
-        def _():
-            for r in range(1, 4):
-                small(0, r).start()
-                small(1, r).start()
+    spread(0)
+    for r in range(1, 4):
+        small(0, r).start()
+        small(1, r).start()
+    forward(0)
+    group(Z_IN, 3).start()
+    spread(1)
+    spread(2)
+
+    def turn(k, carry):
+        @pl.when(k == 1)
+        def _():
+            forward(1)
+            spread(3)
+            forward(2)
+
+        @pl.when(k == 2)
+        def _():
+            forward(3)
+
+        @pl.when(k >= 1)
+        def _():
+            join_cores(k - 1)
+
+        experts(k)
+
+        @pl.when(k >= 2)
+        def _():
+            join_sides(k - 2)
+
+        @pl.when(k >= 1)
+        def _():
+            join_diagonal(k - 1)
 
         return carry
 
-    lax.fori_loop(0, 8, turn, 0)
+    lax.fori_loop(0, 4, turn, 0)
+    join_cores(3)
+    join_sides(2)
+    join_diagonal(3)
+    join_sides(3)
 
     mixed = jnp.zeros((tok, width), jnp.float32)
     eye = lax.broadcasted_iota(jnp.int32, (tok, tok), 0) == lax.broadcasted_iota(

time: 83.4 us -> 75.9 us (0.910)
  Pallas kernels: 79.7 us -> 72.2 us
    pallas_call x1, Pallas kernels: 79.7 us -> 72.2 us  [fused(): pl.pallas_call(fused_kernel, out_shape=(jax.ShapeDtypeStruct(latent.shape...]
where the time goes in v3:
time: 75.9 us; the launch traced here: 75.7 us
  Pallas kernels  72.2 us (95%)
  local copies, waits for them, and re-layouts  2.8 us (4%)
    pallas_call x1, Pallas kernels, fused(): pl.pallas_call(fused_kernel, out_shape=(jax.ShapeDtypeStruct(latent.shape...  72.2 us
    unnamed x2, local copies, waits for them, and re-layouts  2.8 us

profile of v3, /device:TPU:0, one launch (start us, length us, event | category | flops | bytes accessed | tf_op | source)
XLA Modules:
  0.0 75.7 jit_solution(10264784072842493124)
XLA Ops:
  0.6 72.2 %guided_step.1 = (f32[1,32,64]{2,1,0:T(8,128)}, bf16[1,32,1024]{2,1,0:T(8,128)(2,1)}) custom-call(f32[1,32,2048]{2,1,0:T(8,128)} %hid_hbm.1, f32[1,2048]{1,0:T(1,128)} %bitcast.4, s32[1,2,32]{2,1,0:T(2,128)} %bitcast.6, f32[1,2,32]{2,1,0:T(2,128)} %bitcast.7, bf16[1,2048,512]{2,1,0:T(8,128)(2,1)} %gate_hbm.1, bf16[1,2048,512]{2,1,0:T(8,128)(2,1)} %up_hbm.1, ...), custom_call_target="tpu_custom_call" | custom-call | tf_op jit(solution)/shard_map/guided_step/pallas_call | solution.py:633
  72.9 1.3 %copy.17 = f32[1,32,64]{2,1,0:T(8,128)} copy(f32[1,32,64]{2,1,0:T(8,128)} %get-tuple-element.4) | data formatting | bytes 16384
  74.2 1.5 %copy.18 = bf16[1,32,1024]{2,1,0:T(8,128)(2,1)} copy(bf16[1,32,1024]{2,1,0:T(8,128)(2,1)} %get-tuple-element.5) | data formatting | bytes 131072

commit v4 on v3

--- a/solution.py
+++ b/solution.py
@@ -361,7 +361,7 @@
         for r in range(4):
             group(CORE_IN + r, k).wait_recv()
 
-        @pl.when(k == 0)
+        @pl.when(k == 1)
         def _():
             for load in loads[:3]:
                 load.wait()
@@ -430,38 +430,39 @@
     spread(1)
     spread(2)
 
-    def turn(k, carry):
-        @pl.when(k == 1)
-        def _():
-            forward(1)
+    forward(1)
+
+    def turn(i, carry):
+        @pl.when(i == 1)
+        def _():
             spread(3)
             forward(2)
 
-        @pl.when(k == 2)
+        @pl.when(i == 2)
         def _():
             forward(3)
 
-        @pl.when(k >= 1)
-        def _():
-            join_cores(k - 1)
-
-        experts(k)
-
-        @pl.when(k >= 2)
-        def _():
-            join_sides(k - 2)
-
-        @pl.when(k >= 1)
-        def _():
-            join_diagonal(k - 1)
+        @pl.when(i >= 1)
+        def _():
+            join_cores(i)
+
+        experts(lax.rem(i + 1, 4))
+
+        @pl.when(i >= 2)
+        def _():
+            join_sides(i - 1)
+
+        @pl.when(i >= 1)
+        def _():
+            join_diagonal(i)
 
         return carry
 
     lax.fori_loop(0, 4, turn, 0)
-    join_cores(3)
-    join_sides(2)
-    join_diagonal(3)
+    join_cores(0)
     join_sides(3)
+    join_diagonal(0)
+    join_sides(0)
 
     mixed = jnp.zeros((tok, width), jnp.float32)
     eye = lax.broadcasted_iota(jnp.int32, (tok, tok), 0) == lax.broadcasted_iota(

time: 75.9 us -> 81.4 us (1.072)
  Pallas kernels: 72.2 us -> 77.8 us
    pallas_call x1, Pallas kernels: 72.2 us -> 77.8 us  [fused(): pl.pallas_call(fused_kernel, out_shape=(jax.ShapeDtypeStruct(latent.shape...]
where the time goes in v4:
time: 81.4 us; the launch traced here: 81.2 us
  Pallas kernels  77.8 us (96%)
  local copies, waits for them, and re-layouts  2.8 us (3%)
    pallas_call x1, Pallas kernels, fused(): pl.pallas_call(fused_kernel, out_shape=(jax.ShapeDtypeStruct(latent.shape...  77.8 us
    unnamed x2, local copies, waits for them, and re-layouts  2.8 us

profile of v4, /device:TPU:0, one launch (start us, length us, event | category | flops | bytes accessed | tf_op | source)
XLA Modules:
  0.0 81.2 jit_solution(13596372245053391180)
XLA Ops:
  0.6 77.8 %guided_step.1 = (f32[1,32,64]{2,1,0:T(8,128)}, bf16[1,32,1024]{2,1,0:T(8,128)(2,1)}) custom-call(f32[1,32,2048]{2,1,0:T(8,128)} %hid_hbm.1, f32[1,2048]{1,0:T(1,128)} %bitcast.4, s32[1,2,32]{2,1,0:T(2,128)} %bitcast.6, f32[1,2,32]{2,1,0:T(2,128)} %bitcast.7, bf16[1,2048,512]{2,1,0:T(8,128)(2,1)} %gate_hbm.1, bf16[1,2048,512]{2,1,0:T(8,128)(2,1)} %up_hbm.1, ...), custom_call_target="tpu_custom_call" | custom-call | tf_op jit(solution)/shard_map/guided_step/pallas_call | solution.py:634
  78.4 1.3 %copy.17 = f32[1,32,64]{2,1,0:T(8,128)} copy(f32[1,32,64]{2,1,0:T(8,128)} %get-tuple-element.4) | data formatting | bytes 16384
  79.7 1.5 %copy.18 = bf16[1,32,1024]{2,1,0:T(8,128)(2,1)} copy(bf16[1,32,1024]{2,1,0:T(8,128)(2,1)} %get-tuple-element.5) | data formatting | bytes 131072
